TPU v7x, 32 devices: a whole 2x2x4 slice. The times are simulated.
32 devices in a mesh: group: 4 (over y, x), blk: 8 (over z, core).
Axes of the slice: x: 2, y: 2, z: 4, core: 2. Of those that a mesh axis runs over, the one named last changes fastest.
Arguments:
- embeddings: float32 [18432, 1024], P(('group', 'blk')), may hold values from -100 to 100
- cluster: int32 [18432], P(('group', 'blk')), may hold values from 0 to 63, as said below
- global_index: int32 [18432], P(('group', 'blk')), may hold values from 0 to 18431, each once
- send_counts: int32 [32, 4], P(('group', 'blk')), may hold values from 1 to 216, as said below
Outputs:
- best_cosine: float32 [18432], P(('group', 'blk'))
Inputs may be any that keep to these rules, and one draw needn't show every extreme that they name: The row's cluster group is given by send_counts; of the rows that one device sends to one cluster group, at most 27 have a cluster number in any one block c // 8 of consecutive cluster numbers, and every device has exactly 27 in some block. `global_index`: each number once over all devices. The 4 counts of a device sum to 576; its rows stand in order of cluster group, send_counts[d,g] of them for group g; every device has a count of exactly 216.
All inputs are finite; a program needn't handle non-finite values.
Results may differ from a plain program's by a relative error of at most 0.0003.
Values may be sent and summed in bfloat16 or wider, within the bound.
A program may use at most 128 MiB of HBM per device.

v0:
```python
import functools

import jax
import jax.numpy as jnp
from jax import lax
from jax.experimental import pallas as pl
from jax.experimental.pallas import tpu as pltpu
from jax.sharding import PartitionSpec as P

CLUSTERS = 64
SUB = 16
SPAN = 32
TILE = 256
MESH = pl.DeviceIdType.MESH
NT = (((1,), (1,)), ((), ()))
TN = (((0,), (0,)), ((), ()))
F32 = jnp.float32
BF16 = jnp.bfloat16


def iota(shape, dim):
    return lax.broadcasted_iota(jnp.int32, shape, dim)


def hot_of(mask):
    return mask.astype(F32).astype(BF16)


def kernel(groups, blocks, full, tail, keep, high, cnt_hbm, cl_hbm, gid_hbm, emb_hbm, out_ref,
           cnt_ref, cl_ref, gid_ref, emb_ref, packed, recv, unit, late, back, home,
           in_sem, send_sem, recv_sem, bsend_sem, brecv_sem, self_sem):
    rows, width = emb_ref.shape
    n = groups * blocks
    band = n * SUB
    parts = full + 1
    per_block = CLUSTERS // blocks
    lows = blocks // 2
    rest = width - keep
    per = keep // rest if rest else 1
    shift = full * width
    my_g = lax.axis_index("group")
    my_b = lax.axis_index("blk")
    my_hi, my_lo = my_b // lows, lax.rem(my_b, lows)
    me = my_g * blocks + my_b

    def peer(i, way):
        hi = lax.rem(my_hi + 1 - i // (n // 2), 2)
        j = lax.rem(i, n // 2)
        dl, dg = j // groups, lax.rem(j, groups)
        if way < 0:
            dl, dg = lows - dl, groups - dg
        lo = lax.rem(my_lo + dl, lows)
        g = lax.rem(my_g + dg, groups)
        return g, hi * lows + lo

    def others(act, lo=0, hi=None):
        hi = n if hi is None else hi

        def body(i, c):
            act(i)
            return c

        if lo < n // 2:
            lax.fori_loop(lo, min(hi, n // 2), body, 0)
        if hi > n // 2 + 1:
            lax.fori_loop(max(lo, n // 2 + 1), hi, body, 0)

    loads = [
        pltpu.make_async_copy(a, b, in_sem.at[k])
        for k, (a, b) in enumerate(
            ((cnt_hbm, cnt_ref), (cl_hbm, cl_ref), (gid_hbm, gid_ref), (emb_hbm, emb_ref)))
    ]
    for load in loads:
        load.start()

    barrier = pltpu.get_barrier_semaphore()

    def greet(i):
        g, b = peer(i, 1)
        pl.semaphore_signal(barrier, inc=1, device_id={"group": g, "blk": b}, device_id_type=MESH)

    others(greet)

    for load in loads[:3]:
        load.wait()
    pos = iota((1, rows), 1)
    owner = jnp.zeros((1, rows), jnp.int32)
    end = jnp.zeros((1, 1), jnp.int32)
    for g in range(groups - 1):
        end = end + cnt_ref[0:1, g:g + 1]
        owner += (pos >= end).astype(jnp.int32)
    cl = cl_ref[...].reshape(1, rows)
    gid = gid_ref[...].reshape(1, rows)
    to_b = cl // per_block
    to_hi, to_lo = to_b // lows, to_b % lows
    step = (
        jnp.where(to_hi == my_hi, n // 2, 0)
        + ((to_lo + lows - my_lo) % lows) * groups
        + (owner + groups - my_g) % groups
    )
    hot = (iota((n, rows), 0) == step).astype(F32)
    hot_b = hot.astype(BF16)
    upper = hot_of(iota((rows, rows), 0) < iota((rows, rows), 1))
    before = jnp.dot(hot_b, upper, preferred_element_type=F32)
    rank = jnp.sum(hot * before, axis=0, keepdims=True).astype(jnp.int32)
    u = rank - full * SUB
    first = step * SUB

    digits = (
        (cl % per_block + 1) * high + gid // 65536,
        (gid // 256) % 256,
        gid % 256,
    )
    lane = iota((128, rows), 0)
    spots = jnp.zeros((128, rows), F32)
    for k, d in enumerate(digits):
        spots = jnp.where(lane == rank + k * SPAN, d.astype(F32), spots)
    meta = lax.dot_general(hot_b, spots.astype(BF16), NT, preferred_element_type=F32).astype(BF16)

    slots = [jnp.where(rank // SUB == p, first + rank % SUB, -1) for p in range(full)]
    slots.append(jnp.where(u >= 0, first + u, -1))
    if rest:
        slots += [jnp.where((u >= 0) & (u % per == j), first + tail + u // per, -1) for j in range(per)]

    loads[3].wait()
    x = emb_ref[...]
    squares = jnp.sum(x * x, axis=1, keepdims=True)
    unit[...] = (x * lax.rsqrt(squares + 1e-06)).astype(BF16)

    mine = pl.ds(pl.multiple_of(me * SUB, SUB), SUB)

    def out_copy(i):
        g, b = peer(i, 1)
        return pltpu.make_async_remote_copy(
            src_ref=packed.at[pl.ds(pl.multiple_of(i * SUB, SUB), SUB)],
            dst_ref=recv.at[mine],
            send_sem=send_sem, recv_sem=recv_sem,
            device_id={"group": g, "blk": b}, device_id_type=MESH,
        )

    for t in range(band // TILE):
        rows_t = slice(t * TILE, (t + 1) * TILE)
        at_row = iota((TILE, rows), 0) + t * TILE
        for p in range(full):
            packed[rows_t, p * width:(p + 1) * width] = jnp.dot(
                hot_of(at_row == slots[p]), unit[...], preferred_element_type=F32).astype(BF16)
        last = jnp.dot(hot_of(at_row == slots[full]), unit[:, :keep], preferred_element_type=F32)
        if rest:
            extra = [
                jnp.dot(hot_of(at_row == slots[full + 1 + j]), unit[:, keep:], preferred_element_type=F32)
                for j in range(per)
            ]
            last += jnp.concatenate(extra, axis=1)
        where = hot_of(iota((TILE, n), 0) + t * TILE == iota((TILE, n), 1) * SUB + SUB - 1)
        info = jnp.dot(where, meta, preferred_element_type=F32)
        packed[rows_t, shift:shift + 128] = (last[:, :128] + info).astype(BF16)
        packed[rows_t, shift + 128:shift + keep] = last[:, 128:].astype(BF16)
        if t == 0:
            pl.semaphore_wait(barrier, n - 1)
        others(lambda i: out_copy(i).start(), t * TILE // SUB, (t + 1) * TILE // SUB)

    own = pltpu.make_async_copy(packed.at[pl.ds(band // 2, SUB)], recv.at[mine], self_sem)
    own.start()
    own.wait()

    def all_rows():
        g, b = peer(0, 1)
        most = pl.ds(0, (n - 1) * SUB)
        return pltpu.make_async_remote_copy(
            src_ref=packed.at[most], dst_ref=recv.at[most], send_sem=send_sem, recv_sem=recv_sem,
            device_id={"group": g, "blk": b}, device_id_type=MESH)

    all_rows().wait_recv()

    total = parts * band
    take = hot_of(iota((n, band), 1) == iota((n, band), 0) * SUB + SUB - 1)
    info = jnp.dot(take, recv[:, shift:shift + 128], preferred_element_type=F32)
    which = iota((n, 128), 1) // SPAN
    info = jnp.concatenate([jnp.where(which == k, info, 0.0) for k in range(3)], axis=0).astype(BF16)
    at = iota((128, total), 1)
    spread = hot_of(iota((128, total), 0) % SPAN == at // band * SUB + at % SUB)
    wide = jnp.dot(info, spread, preferred_element_type=F32)
    source = (iota((n, total), 1) % band) // SUB == iota((n, total), 0)
    d0, d1, d2 = (
        jnp.sum(jnp.where(source, wide[k * n:(k + 1) * n], 0.0), axis=0, keepdims=True) for k in range(3)
    )
    key_row = d0 * 65536.0 + d1 * 256.0 + d2
    low_row = jnp.floor(d0 * (1.0 / high)) * (high * 65536.0)
    key_col = jnp.transpose(jnp.broadcast_to(key_row, (8, total)))[:, 0:1]

    late[:, :keep] = recv[:, shift:shift + keep]
    if rest:
        a, b = iota((TILE, TILE), 0), iota((TILE, TILE), 1)
        v = a % SUB
        for t in range(band // TILE):
            rows_t = slice(t * TILE, (t + 1) * TILE)
            found = jnp.zeros((TILE, rest), F32)
            for j in range(per):
                pick = (a // SUB == b // SUB) & (v < tail) & (v % per == j) & (b % SUB == tail + v // per)
                found += jnp.dot(
                    hot_of(pick), recv[rows_t, shift + j * rest:shift + (j + 1) * rest],
                    preferred_element_type=F32)
            late[rows_t, keep:] = found.astype(BF16)

    def part(p, lo, hi):
        return recv[lo:hi, p * width:(p + 1) * width] if p < full else late[lo:hi, :]

    for t in range(total // TILE):
        lanes = slice(t * TILE, (t + 1) * TILE)
        p, lo = t * TILE // band, t * TILE % band
        query = part(p, lo, lo + TILE)
        best = jnp.full((1, TILE), -1.0, F32)
        for q in range(parts):
            cosine = lax.dot_general(part(q, 0, band), query, NT, preferred_element_type=F32)
            keys = key_col[q * band:(q + 1) * band]
            usable = (keys >= low_row[:, lanes]) & (keys < key_row[:, lanes])
            best = jnp.maximum(best, jnp.max(jnp.where(usable, cosine, -1.0), axis=0, keepdims=True))
        for w in range(TILE // 128):
            back[lo // 128 + w, p:p + 1, :] = best[:, w * 128:(w + 1) * 128]

    def back_copy(i):
        g, b = peer(i, -1)
        return pltpu.make_async_remote_copy(
            src_ref=back.at[((g * blocks + b) * SUB) // 128], dst_ref=home.at[i],
            send_sem=bsend_sem, recv_sem=brecv_sem,
            device_id={"group": g, "blk": b}, device_id_type=MESH,
        )

    others(lambda i: back_copy(i).start())
    own_back = pltpu.make_async_copy(back.at[(me * SUB) // 128], home.at[n // 2], self_sem)
    own_back.start()
    own_back.wait()

    def all_back():
        g, b = peer(0, -1)
        most = home.at[pl.ds(0, n - 1)]
        return pltpu.make_async_remote_copy(
            src_ref=most, dst_ref=most, send_sem=bsend_sem, recv_sem=brecv_sem,
            device_id={"group": g, "blk": b}, device_id_type=MESH)

    all_back().wait_recv()

    found = jnp.zeros((128, rows), F32)
    for p in range(parts):
        found += lax.dot_general(
            home[:, p, :], jnp.where(rank // SUB == p, hot, 0.0), TN,
            precision=lax.Precision.HIGHEST, preferred_element_type=F32)
    off = lax.rem(me * SUB, 128)
    result = jnp.sum(jnp.where(lane == rank % SUB + off, found, 0.0), axis=0, keepdims=True)
    out_ref[...] = result.reshape(rows)
    all_rows().wait_send()
    all_back().wait_send()


def on_device(embeddings, cluster, global_index, send_counts):
    rows, width = embeddings.shape
    groups = lax.axis_size("group")
    blocks = lax.axis_size("blk")
    n = groups * blocks
    capacity = -(-(3 * rows // (2 * groups)) // blocks)
    full, tail = capacity // SUB, capacity % SUB
    for keep in (width // 2, 3 * width // 4, width):
        rest = width - keep
        if tail + (-(-tail // (keep // rest)) if rest else 0) < SUB:
            break
    high = (n * rows - 1) // 65536 + 1
    band = n * SUB
    lanes = full * width + keep
    anywhere = pl.BlockSpec(memory_space=pltpu.HBM)
    return pl.pallas_call(
        functools.partial(kernel, groups, blocks, full, tail, keep, high),
        out_shape=jax.ShapeDtypeStruct((rows,), F32),
        in_specs=[anywhere] * 4,
        out_specs=pl.BlockSpec(memory_space=pltpu.VMEM),
        scratch_shapes=[
            pltpu.VMEM((1, groups), jnp.int32),
            pltpu.VMEM((rows,), jnp.int32),
            pltpu.VMEM((rows,), jnp.int32),
            pltpu.VMEM((rows, width), F32),
            pltpu.VMEM((band, lanes), BF16),
            pltpu.VMEM((band, lanes), BF16),
            pltpu.VMEM((rows, width), BF16),
            pltpu.VMEM((band, width), BF16),
            pltpu.VMEM((band // 128, full + 1, 128), F32),
            pltpu.VMEM((n, full + 1, 128), F32),
            pltpu.SemaphoreType.DMA((4,)),
            pltpu.SemaphoreType.DMA,
            pltpu.SemaphoreType.DMA,
            pltpu.SemaphoreType.DMA,
            pltpu.SemaphoreType.DMA,
            pltpu.SemaphoreType.DMA,
        ],
        compiler_params=pltpu.CompilerParams(
            collective_id=0, has_side_effects=True, vmem_limit_bytes=48 * 1024 * 1024
        ),
    )(send_counts, cluster, global_index, embeddings)


def solution(mesh):
    placed = (
        P(("group", "blk"), None),
        P(("group", "blk")),
        P(("group", "blk")),
        P(("group", "blk"), None),
    )
    return jax.shard_map(
        on_device, mesh=mesh, in_specs=placed, out_specs=P(("group", "blk")), check_vma=False
    )
```

profile of v0, /device:TPU:0, one launch (start us, length us, event | category | flops | bytes accessed | tf_op | source)
XLA Modules:
  0.0 62.1 jit_solution(14444838234286599127)
XLA Ops:
  0.0 0.0 copy-start
  0.0 1.7 %copy-done = f32[576,1024]{1,0:T(8,128)S(1)} copy-done((f32[576,1024]{1,0:T(8,128)S(1)}, f32[576,1024]{1,0:T(8,128)}, u32[]{:S(2)}) %copy-start) | copy-done | bytes 2359320
  1.7 0.0 copy-start.1
  1.7 0.7 %copy-done.1 = s32[576]{0:T(1024)S(1)} copy-done((s32[576]{0:T(1024)S(1)}, s32[576]{0:T(1024)}, u32[]{:S(2)}) %copy-start.1) | copy-done | bytes 2328
  2.4 0.0 copy-start.2
  2.4 0.7 %copy-done.2 = s32[576]{0:T(1024)S(1)} copy-done((s32[576]{0:T(1024)S(1)}, s32[576]{0:T(1024)}, u32[]{:S(2)}) %copy-start.2) | copy-done | bytes 2328
  3.0 0.0 copy-start.3
  3.0 0.7 %copy-done.3 = s32[1,4]{1,0:T(1,128)S(1)} copy-done((s32[1,4]{1,0:T(1,128)S(1)}, s32[1,4]{1,0:T(1,128)}, u32[]{:S(2)}) %copy-start.3) | copy-done | bytes 40
  3.7 57.8 %shard_map.46 = f32[576]{0:T(1024)S(1)} custom-call(s32[1,4]{1,0:T(1,128)S(1)} %copy-done.3, s32[576]{0:T(1024)S(1)} %copy-done.1, s32[576]{0:T(1024)S(1)} %copy-done.2, f32[576,1024]{1,0:T(8,128)S(1)} %copy-done), custom_call_target="tpu_custom_call" | custom-call | tf_op jit(solution)/shard_map/pallas_call | solution.py:270
  61.5 0.6 copy.6
Async XLA Ops:
  0.0 1.7 %copy-start = (f32[576,1024]{1,0:T(8,128)S(1)}, f32[576,1024]{1,0:T(8,128)}, u32[]{:S(2)}) copy-start(f32[576,1024]{1,0:T(8,128)} %emb_hbm.1) | copy-start | bytes 7077892
  1.7 0.7 %copy-start.1 = (s32[576]{0:T(1024)S(1)}, s32[576]{0:T(1024)}, u32[]{:S(2)}) copy-start(s32[576]{0:T(1024)} %cl_hbm.1) | copy-start | bytes 6916
  2.4 0.7 %copy-start.2 = (s32[576]{0:T(1024)S(1)}, s32[576]{0:T(1024)}, u32[]{:S(2)}) copy-start(s32[576]{0:T(1024)} %gid_hbm.1) | copy-start | bytes 6916
  3.0 0.7 %copy-start.3 = (s32[1,4]{1,0:T(1,128)S(1)}, s32[1,4]{1,0:T(1,128)}, u32[]{:S(2)}) copy-start(s32[1,4]{1,0:T(1,128)} %cnt_hbm.1) | copy-start | bytes 52
where the time goes:
time: 62.3 us; the launch traced here: 62.1 us
  Pallas kernels  57.8 us (93%)
  local copies, waits for them, and re-layouts  4.29 us (7%)
    pallas_call x1, Pallas kernels, on_device(): pl.pallas_call(functools.partial(kernel, groups, blocks, full, tail, keep...  57.8 us
    unnamed x9, local copies, waits for them, and re-layouts  4.29 us

commit v1 on v0

--- a/solution.py
+++ b/solution.py
@@ -291,7 +291,7 @@
             pltpu.SemaphoreType.DMA,
         ],
         compiler_params=pltpu.CompilerParams(
-            collective_id=0, has_side_effects=True, vmem_limit_bytes=48 * 1024 * 1024
+            collective_id=0, has_side_effects=True, vmem_limit_bytes=63 * 1024 * 1024
         ),
     )(send_counts, cluster, global_index, embeddings)
 

time: 62.3 us -> 59.5 us (0.955)
  local copies, waits for them, and re-layouts: 4.29 us -> 1.28 us
    unnamed x9 -> x1, local copies, waits for them, and re-layouts: 4.29 us -> 1.28 us
where the time goes in v1:
time: 59.5 us; the launch traced here: 59.3 us
  Pallas kernels  58 us (97%)
  local copies, waits for them, and re-layouts  1.28 us (2%)
    pallas_call x1, Pallas kernels, on_device(): pl.pallas_call(functools.partial(kernel, groups, blocks, full, tail, keep...  58 us
    unnamed x1, local copies, waits for them, and re-layouts  1.28 us

profile of v1, /device:TPU:0, one launch (start us, length us, event | category | flops | bytes accessed | tf_op | source)
XLA Modules:
  0.0 59.3 jit_solution(9026117589076480594)
XLA Ops:
  0.0 58.0 %shard_map.46 = f32[576]{0:T(1024)} custom-call(s32[1,4]{1,0:T(1,128)} %cnt_hbm.1, s32[576]{0:T(1024)} %cl_hbm.1, s32[576]{0:T(1024)} %gid_hbm.1, f32[576,1024]{1,0:T(8,128)} %emb_hbm.1), custom_call_target="tpu_custom_call" | custom-call | tf_op jit(solution)/shard_map/pallas_call | solution.py:270
  58.0 1.3 %copy.6 = f32[576]{0:T(1024)} copy(f32[576]{0:T(1024)} %shard_map.46) | data formatting | bytes 4608

commit v2 on v1

--- a/solution.py
+++ b/solution.py
@@ -41,7 +41,6 @@
     my_g = lax.axis_index("group")
     my_b = lax.axis_index("blk")
     my_hi, my_lo = my_b // lows, lax.rem(my_b, lows)
-    me = my_g * blocks + my_b
 
     def peer(i, way):
         hi = lax.rem(my_hi + 1 - i // (n // 2), 2)
@@ -127,14 +126,18 @@
     squares = jnp.sum(x * x, axis=1, keepdims=True)
     unit[...] = (x * lax.rsqrt(squares + 1e-06)).astype(BF16)
 
-    mine = pl.ds(pl.multiple_of(me * SUB, SUB), SUB)
+    half = band // 2
+    place = my_g * lows + my_lo
+
+    def mine(far):
+        return pl.ds(pl.multiple_of(far * half + place * SUB, SUB), SUB)
 
     def out_copy(i):
         g, b = peer(i, 1)
         return pltpu.make_async_remote_copy(
             src_ref=packed.at[pl.ds(pl.multiple_of(i * SUB, SUB), SUB)],
-            dst_ref=recv.at[mine],
-            send_sem=send_sem, recv_sem=recv_sem,
+            dst_ref=recv.at[mine(i // (n // 2))],
+            send_sem=send_sem, recv_sem=recv_sem.at[i // (n // 2)],
             device_id={"group": g, "blk": b}, device_id_type=MESH,
         )
 
@@ -159,75 +162,96 @@
             pl.semaphore_wait(barrier, n - 1)
         others(lambda i: out_copy(i).start(), t * TILE // SUB, (t + 1) * TILE // SUB)
 
-    own = pltpu.make_async_copy(packed.at[pl.ds(band // 2, SUB)], recv.at[mine], self_sem)
+    own = pltpu.make_async_copy(packed.at[pl.ds(band // 2, SUB)], recv.at[mine(1)], self_sem)
     own.start()
     own.wait()
 
-    def all_rows():
+    def many(count, k):
         g, b = peer(0, 1)
-        most = pl.ds(0, (n - 1) * SUB)
+        most = pl.ds(0, count * SUB)
         return pltpu.make_async_remote_copy(
-            src_ref=packed.at[most], dst_ref=recv.at[most], send_sem=send_sem, recv_sem=recv_sem,
+            src_ref=packed.at[most], dst_ref=recv.at[most], send_sem=send_sem, recv_sem=recv_sem.at[k],
             device_id={"group": g, "blk": b}, device_id_type=MESH)
 
-    all_rows().wait_recv()
-
-    total = parts * band
-    take = hot_of(iota((n, band), 1) == iota((n, band), 0) * SUB + SUB - 1)
-    info = jnp.dot(take, recv[:, shift:shift + 128], preferred_element_type=F32)
-    which = iota((n, 128), 1) // SPAN
-    info = jnp.concatenate([jnp.where(which == k, info, 0.0) for k in range(3)], axis=0).astype(BF16)
-    at = iota((128, total), 1)
-    spread = hot_of(iota((128, total), 0) % SPAN == at // band * SUB + at % SUB)
-    wide = jnp.dot(info, spread, preferred_element_type=F32)
-    source = (iota((n, total), 1) % band) // SUB == iota((n, total), 0)
-    d0, d1, d2 = (
-        jnp.sum(jnp.where(source, wide[k * n:(k + 1) * n], 0.0), axis=0, keepdims=True) for k in range(3)
-    )
-    key_row = d0 * 65536.0 + d1 * 256.0 + d2
-    low_row = jnp.floor(d0 * (1.0 / high)) * (high * 65536.0)
-    key_col = jnp.transpose(jnp.broadcast_to(key_row, (8, total)))[:, 0:1]
-
-    late[:, :keep] = recv[:, shift:shift + keep]
-    if rest:
-        a, b = iota((TILE, TILE), 0), iota((TILE, TILE), 1)
-        v = a % SUB
-        for t in range(band // TILE):
-            rows_t = slice(t * TILE, (t + 1) * TILE)
-            found = jnp.zeros((TILE, rest), F32)
-            for j in range(per):
-                pick = (a // SUB == b // SUB) & (v < tail) & (v % per == j) & (b % SUB == tail + v // per)
-                found += jnp.dot(
-                    hot_of(pick), recv[rows_t, shift + j * rest:shift + (j + 1) * rest],
-                    preferred_element_type=F32)
-            late[rows_t, keep:] = found.astype(BF16)
+    def ready(h):
+        base = h * half
+        m = n // 2
+        total = parts * half
+        take = hot_of(iota((m, half), 1) == iota((m, half), 0) * SUB + SUB - 1)
+        info = jnp.dot(take, recv[base:base + half, shift:shift + 128], preferred_element_type=F32)
+        which = iota((m, 128), 1) // SPAN
+        info = jnp.concatenate([jnp.where(which == k, info, 0.0) for k in range(3)], axis=0).astype(BF16)
+        at = iota((128, total), 1)
+        spread = hot_of(iota((128, total), 0) % SPAN == at // half * SUB + at % SUB)
+        wide = jnp.dot(info, spread, preferred_element_type=F32)
+        source = (iota((m, total), 1) % half) // SUB == iota((m, total), 0)
+        d0, d1, d2 = (
+            jnp.sum(jnp.where(source, wide[k * m:(k + 1) * m], 0.0), axis=0, keepdims=True)
+            for k in range(3)
+        )
+        key_row = d0 * 65536.0 + d1 * 256.0 + d2
+        low_row = jnp.floor(d0 * (1.0 / high)) * (high * 65536.0)
+        key_col = jnp.transpose(jnp.broadcast_to(key_row, (8, total)))[:, 0:1]
+        late[base:base + half, :keep] = recv[base:base + half, shift:shift + keep]
+        if rest:
+            a, b = iota((TILE, TILE), 0), iota((TILE, TILE), 1)
+            v = a % SUB
+            for t in range(half // TILE):
+                rows_t = slice(base + t * TILE, base + (t + 1) * TILE)
+                found = jnp.zeros((TILE, rest), F32)
+                for j in range(per):
+                    pick = (a // SUB == b // SUB) & (v < tail) & (v % per == j) & (b % SUB == tail + v // per)
+                    found += jnp.dot(
+                        hot_of(pick), recv[rows_t, shift + j * rest:shift + (j + 1) * rest],
+                        preferred_element_type=F32)
+                late[rows_t, keep:] = found.astype(BF16)
+        return key_row, low_row, key_col
 
     def part(p, lo, hi):
         return recv[lo:hi, p * width:(p + 1) * width] if p < full else late[lo:hi, :]
 
-    for t in range(total // TILE):
-        lanes = slice(t * TILE, (t + 1) * TILE)
-        p, lo = t * TILE // band, t * TILE % band
-        query = part(p, lo, lo + TILE)
-        best = jnp.full((1, TILE), -1.0, F32)
-        for q in range(parts):
-            cosine = lax.dot_general(part(q, 0, band), query, NT, preferred_element_type=F32)
-            keys = key_col[q * band:(q + 1) * band]
-            usable = (keys >= low_row[:, lanes]) & (keys < key_row[:, lanes])
-            best = jnp.maximum(best, jnp.max(jnp.where(usable, cosine, -1.0), axis=0, keepdims=True))
+    known = {}
+    tiles = half // TILE
+    bests = {}
+
+    def meet(hq, hk):
+        key_row, low_row = known[hq][0], known[hq][1]
+        key_col = known[hk][2]
+        for p in range(parts):
+            for t in range(tiles):
+                query = part(p, hq * half + t * TILE, hq * half + (t + 1) * TILE)
+                lanes = slice(p * half + t * TILE, p * half + (t + 1) * TILE)
+                best = bests.get((hq, p, t), jnp.full((1, TILE), -1.0, F32))
+                for q in range(parts):
+                    cosine = lax.dot_general(
+                        part(q, hk * half, (hk + 1) * half), query, NT, preferred_element_type=F32)
+                    keys = key_col[q * half:(q + 1) * half]
+                    usable = (keys >= low_row[:, lanes]) & (keys < key_row[:, lanes])
+                    best = jnp.maximum(best, jnp.max(jnp.where(usable, cosine, -1.0), axis=0, keepdims=True))
+                bests[(hq, p, t)] = best
+
+    many(n // 2 - 1, 1).wait_recv()
+    known[1] = ready(1)
+    meet(1, 1)
+    many(n // 2, 0).wait_recv()
+    known[0] = ready(0)
+    meet(0, 0)
+    meet(0, 1)
+    meet(1, 0)
+    for (h, p, t), best in bests.items():
         for w in range(TILE // 128):
-            back[lo // 128 + w, p:p + 1, :] = best[:, w * 128:(w + 1) * 128]
+            back[(h * half + t * TILE) // 128 + w, p:p + 1, :] = best[:, w * 128:(w + 1) * 128]
 
     def back_copy(i):
         g, b = peer(i, -1)
         return pltpu.make_async_remote_copy(
-            src_ref=back.at[((g * blocks + b) * SUB) // 128], dst_ref=home.at[i],
+            src_ref=back.at[(i // (n // 2) * half + (g * lows + lax.rem(b, lows)) * SUB) // 128], dst_ref=home.at[i],
             send_sem=bsend_sem, recv_sem=brecv_sem,
             device_id={"group": g, "blk": b}, device_id_type=MESH,
         )
 
     others(lambda i: back_copy(i).start())
-    own_back = pltpu.make_async_copy(back.at[(me * SUB) // 128], home.at[n // 2], self_sem)
+    own_back = pltpu.make_async_copy(back.at[(half + place * SUB) // 128], home.at[n // 2], self_sem)
     own_back.start()
     own_back.wait()
 
@@ -245,10 +269,10 @@
         found += lax.dot_general(
             home[:, p, :], jnp.where(rank // SUB == p, hot, 0.0), TN,
             precision=lax.Precision.HIGHEST, preferred_element_type=F32)
-    off = lax.rem(me * SUB, 128)
+    off = lax.rem(place * SUB, 128)
     result = jnp.sum(jnp.where(lane == rank % SUB + off, found, 0.0), axis=0, keepdims=True)
     out_ref[...] = result.reshape(rows)
-    all_rows().wait_send()
+    many(n - 1, 0).wait_send()
     all_back().wait_send()
 
 
@@ -285,7 +309,7 @@
             pltpu.VMEM((n, full + 1, 128), F32),
             pltpu.SemaphoreType.DMA((4,)),
             pltpu.SemaphoreType.DMA,
-            pltpu.SemaphoreType.DMA,
+            pltpu.SemaphoreType.DMA((2,)),
             pltpu.SemaphoreType.DMA,
             pltpu.SemaphoreType.DMA,
             pltpu.SemaphoreType.DMA,

time: 59.5 us -> 58.7 us (0.987)
  Pallas kernels: 58 us -> 57.3 us
    pallas_call x1, Pallas kernels: 58 us -> 57.3 us  [on_device(): pl.pallas_call(functools.partial(kernel, groups, blocks, full, tail, keep...]
where the time goes in v2:
time: 58.7 us; the launch traced here: 58.5 us
  Pallas kernels  57.3 us (98%)
  local copies, waits for them, and re-layouts  1.28 us (2%)
    pallas_call x1, Pallas kernels, on_device(): pl.pallas_call(functools.partial(kernel, groups, blocks, full, tail, keep...  57.3 us
    unnamed x1, local copies, waits for them, and re-layouts  1.28 us

profile of v2, /device:TPU:0, one launch (start us, length us, event | category | flops | bytes accessed | tf_op | source)
XLA Modules:
  0.0 58.5 jit_solution(13270010353265035667)
XLA Ops:
  0.0 57.3 %shard_map.46 = f32[576]{0:T(1024)} custom-call(s32[1,4]{1,0:T(1,128)} %cnt_hbm.1, s32[576]{0:T(1024)} %cl_hbm.1, s32[576]{0:T(1024)} %gid_hbm.1, f32[576,1024]{1,0:T(8,128)} %emb_hbm.1), custom_call_target="tpu_custom_call" | custom-call | tf_op jit(solution)/shard_map/pallas_call | solution.py:294
  57.3 1.3 %copy.6 = f32[576]{0:T(1024)} copy(f32[576]{0:T(1024)} %shard_map.46) | data formatting | bytes 4608

commit v3 on v2

--- a/solution.py
+++ b/solution.py
@@ -230,6 +230,20 @@
                     best = jnp.maximum(best, jnp.max(jnp.where(usable, cosine, -1.0), axis=0, keepdims=True))
                 bests[(hq, p, t)] = best
 
+    def keep_best(half_no):
+        for (h, p, t), best in bests.items():
+            if h == half_no:
+                for w in range(TILE // 128):
+                    back[(h * half + t * TILE) // 128 + w, p:p + 1, :] = best[:, w * 128:(w + 1) * 128]
+
+    def back_copy(i):
+        g, b = peer(i, -1)
+        return pltpu.make_async_remote_copy(
+            src_ref=back.at[(i // (n // 2) * half + (g * lows + lax.rem(b, lows)) * SUB) // 128], dst_ref=home.at[i],
+            send_sem=bsend_sem, recv_sem=brecv_sem,
+            device_id={"group": g, "blk": b}, device_id_type=MESH,
+        )
+
     many(n // 2 - 1, 1).wait_recv()
     known[1] = ready(1)
     meet(1, 1)
@@ -237,20 +251,11 @@
     known[0] = ready(0)
     meet(0, 0)
     meet(0, 1)
+    keep_best(0)
+    others(lambda i: back_copy(i).start(), 0, n // 2)
     meet(1, 0)
-    for (h, p, t), best in bests.items():
-        for w in range(TILE // 128):
-            back[(h * half + t * TILE) // 128 + w, p:p + 1, :] = best[:, w * 128:(w + 1) * 128]
-
-    def back_copy(i):
-        g, b = peer(i, -1)
-        return pltpu.make_async_remote_copy(
-            src_ref=back.at[(i // (n // 2) * half + (g * lows + lax.rem(b, lows)) * SUB) // 128], dst_ref=home.at[i],
-            send_sem=bsend_sem, recv_sem=brecv_sem,
-            device_id={"group": g, "blk": b}, device_id_type=MESH,
-        )
-
-    others(lambda i: back_copy(i).start())
+    keep_best(1)
+    others(lambda i: back_copy(i).start(), n // 2, n)
     own_back = pltpu.make_async_copy(back.at[(half + place * SUB) // 128], home.at[n // 2], self_sem)
     own_back.start()
     own_back.wait()

time: 58.7 us -> 58.4 us (level)
  no operation moved by 1% of the time
where the time goes in v3:
time: 58.4 us; the launch traced here: 58.3 us
  Pallas kernels  57 us (98%)
  local copies, waits for them, and re-layouts  1.28 us (2%)
    pallas_call x1, Pallas kernels, on_device(): pl.pallas_call(functools.partial(kernel, groups, blocks, full, tail, keep...  57 us
    unnamed x1, local copies, waits for them, and re-layouts  1.28 us

profile of v3, /device:TPU:0, one launch (start us, length us, event | category | flops | bytes accessed | tf_op | source)
XLA Modules:
  0.0 58.3 jit_solution(12475586951284503577)
XLA Ops:
  0.0 57.0 %shard_map.46 = f32[576]{0:T(1024)} custom-call(s32[1,4]{1,0:T(1,128)} %cnt_hbm.1, s32[576]{0:T(1024)} %cl_hbm.1, s32[576]{0:T(1024)} %gid_hbm.1, f32[576,1024]{1,0:T(8,128)} %emb_hbm.1), custom_call_target="tpu_custom_call" | custom-call | tf_op jit(solution)/shard_map/pallas_call | solution.py:299
  57.0 1.3 %copy.6 = f32[576]{0:T(1024)} copy(f32[576]{0:T(1024)} %shard_map.46) | data formatting | bytes 4608
